TPU v7x, 32 devices: a whole 2x2x4 slice. The times are simulated.
32 devices in a mesh: patch: 8 (over z, y), probe: 4 (over x, core).
Axes of the slice: x: 2, y: 2, z: 4, core: 2. Of those that a mesh axis runs over, the one named last changes fastest.
Arguments:
- probe_columns: bfloat16 [16384, 512], P('patch', 'probe'), may hold values from -6 to 6
- near_field: bfloat16 [128, 16, 128, 128], P('patch')
- column_ids: int32 [128, 16], P('patch'), may hold values from 0 to 127, as said below
- block_counts: int32 [128], P('patch'), may hold values from 1 to 16, as said below
- sketch_matrix: bfloat16 [512, 256], replicated, may hold values from -0.25 to 0.25
Outputs:
- sample: bfloat16 [16384, 512], P('patch', 'probe')
- row_basis: float32 [256, 16384], P('probe', 'patch')
Inputs may be any that keep to these rules, and one draw needn't show every extreme that they name: column_ids[b, 0] = b; every column_ids[b, n] is a row block of the patch device that owns b or of one of the 2 patch devices before or after it. `block_counts`: the number of live slots differs strongly from patch device to patch device.
All inputs are finite; a program needn't handle non-finite values.
Results may differ from a plain program's by a relative error of at most 0.0032.
Values may be sent and summed in bfloat16 or wider, within the bound.
A program may use at most 64 MiB of HBM per device.

v0:
```python
import math

import jax
import jax.numpy as jnp
from jax import lax
from jax.sharding import PartitionSpec as P

REACH = 2


def passed_along(value, axis, steps):
    count = lax.axis_size(axis)
    initial, last = (max(0, -steps), min(count, count - steps))
    return lax.ppermute(value, axis, [(source, source + steps) for source in range(initial, last)])


def partner_2(value, axis, bit):
    mask = 2**bit
    pairs = [(source, source ^ mask) for source in range(lax.axis_size(axis))]
    return lax.ppermute(value, axis, pairs)


def shards(probe_columns, near_field, column_ids, block_counts, sketch_matrix):
    blk_dev = near_field.shape[0]
    slot_count = near_field.shape[1]
    blk_rows = near_field.shape[2]
    row_count, probes_local = probe_columns.shape
    omega_tiles = probe_columns.reshape(blk_dev, blk_rows, probes_local)
    window = []
    for offset in range(-REACH, REACH + 1):
        if offset == 0:
            window.append(omega_tiles)
        else:
            window.append(passed_along(omega_tiles, "patch", -offset))
    window = jnp.concatenate(window, 0)
    first_block = (lax.axis_index("patch") - REACH) * blk_dev
    local_ids = column_ids - first_block
    picked = window[local_ids]
    live_slots = lax.broadcasted_iota(jnp.int32, (blk_dev, slot_count), 1) < block_counts[:, None]
    picked = jnp.where(live_slots[:, :, None, None], picked, jnp.zeros_like(picked))
    product = jnp.einsum("bnrc,bncp->brp", near_field, picked, preferred_element_type=jnp.float32)
    sample = product.reshape(row_count, probes_local).astype(jnp.bfloat16)
    probe_place = lax.axis_index("probe")
    contract = (((0,), (1,)), ((), ()))
    psi_rows = lax.dynamic_slice_in_dim(sketch_matrix, probe_place * probes_local, probes_local, 0)
    factor = lax.psum_scatter(
        lax.dot_general(psi_rows, sample, contract, preferred_element_type=jnp.float32),
        "probe",
        scatter_dimension=0,
        tiled=True,
    )
    highest = lax.Precision.HIGHEST
    gram_local = jnp.dot(factor, factor.T, precision=highest)
    lower = jnp.linalg.cholesky(gram_local)
    for level in range(lax.axis_size("patch").bit_length() - 1):
        partner = partner_2(lower, "patch", level)
        stacked = jnp.dot(lower, lower.T, precision=highest) + jnp.dot(
            partner, partner.T, precision=highest
        )
        lower = jnp.linalg.cholesky(stacked)
    solved = lax.linalg.triangular_solve(lower, factor, left_side=True, lower=True)
    row_basis = solved * math.sqrt(row_count * lax.axis_size("patch"))
    return (sample, row_basis)


def solution(mesh):
    placed = (P("patch", "probe"), P("patch", None, None, None), P("patch", None), P("patch"), P())
    return jax.shard_map(
        shards,
        mesh=mesh,
        in_specs=placed,
        out_specs=(P("patch", "probe"), P("probe", "patch")),
        check_vma=False,
    )
```

profile of v0, /device:TPU:0, one launch (start us, length us, event | category | flops | bytes accessed | tf_op | source)
XLA Modules:
  0.0 150.6 jit_solution(6859887851944997694)
XLA Ops:
  7.2 0.0 copy-start
  7.2 0.0 reduce-scatter.2.cloned.1.call-start
  7.2 5.9 %collective-permute-start = (bf16[16,128,128]{2,1,0:T(8,128)(2,1)}, bf16[16,128,128]{2,1,0:T(8,128)(2,1)}, u32[]{:S(2)}, u32[]{:S(2)}) collective-permute-start(bf16[16,128,128]{2,1,0:T(8,128)(2,1)} %bitcast.49), channel_id=1, source_target_pairs={{0,8},{4,12},{8,16},{12,20},{16,24},{20,28},{1,9},{5,13},{9,17},{1... | collective-permute-start | bytes 1572872 | tf_op jit(solution)/shard_map/ppermute | solution.py:14
  13.1 4.2 %collective-permute-start.1 = (bf16[16,128,128]{2,1,0:T(8,128)(2,1)}, bf16[16,128,128]{2,1,0:T(8,128)(2,1)}, u32[]{:S(2)}, u32[]{:S(2)}) collective-permute-start(bf16[16,128,128]{2,1,0:T(8,128)(2,1)} %bitcast.50), channel_id=1, source_target_pairs={{0,4},{4,8},{8,12},{12,16},{16,20},{20,24},{24,28},{1,5},{5,9},{9,... | collective-permute-start | bytes 1572872 | tf_op jit(solution)/shard_map/ppermute | solution.py:14
  17.3 1.3 collective-permute-start.2
  18.6 1.3 collective-permute-start.3
  19.9 0.7 compare_select_fusion
  20.6 0.7 iota_compare_fusion.2
  21.3 0.1 reshape.39
  21.4 2.3 %collective-permute-done = bf16[16,128,128]{2,1,0:T(8,128)(2,1)} collective-permute-done((bf16[16,128,128]{2,1,0:T(8,128)(2,1)}, bf16[16,128,128]{2,1,0:T(8,128)(2,1)}, u32[]{:S(2)}, u32[]{:S(2)}) %collective-permute-start) | collective-permute-done | bytes 524320 | tf_op jit(solution)/shard_map/ppermute | solution.py:14
  23.8 1.1 constant_dynamic-update-slice_fusion.4
  24.9 14.1 %collective-permute-done.1 = bf16[16,128,128]{2,1,0:T(8,128)(2,1)} collective-permute-done((bf16[16,128,128]{2,1,0:T(8,128)(2,1)}, bf16[16,128,128]{2,1,0:T(8,128)(2,1)}, u32[]{:S(2)}, u32[]{:S(2)}) %collective-permute-start.1) | collective-permute-done | bytes 524320 | tf_op jit(solution)/shard_map/ppermute | solution.py:14
  38.9 1.1 constant_dynamic-update-slice_fusion.3
  40.1 1.1 constant_dynamic-update-slice_fusion.2
  41.2 0.0 collective-permute-done.2
  41.2 1.1 constant_dynamic-update-slice_fusion.1
  42.3 0.8 collective-permute-done.3
  43.2 0.1 constant_dynamic-update-slice_fusion
  43.3 8.6 %gather_fusion = bf16[256,128,128]{2,1,0:T(8,128)(2,1)} fusion(bf16[80,128,128]{2,1,0:T(8,128)(2,1)S(1)} %constant_dynamic-update-slice_fusion, s32[1024]{0:T(1024)S(1)} %pad_clamp_fusion), kind=kCustom, calls=%fused_computation | custom fusion | bytes 16778240 | tf_op jit(solution)/shard_map/gather | solution.py:38
  51.9 8.2 %fusion.7 = bf16[16,128,128]{1,2,0:T(8,128)(2,1)S(1)} fusion(bf16[16,16,128,128]{3,2,1,0:T(8,128)(2,1)} %param.7, bf16[16,16,128,128]{3,2,1,0:T(8,128)(2,1)} %bitcast.48, pred[16,16]{1,0:T(8,128)(4,1)S(1)} %iota_compare_fusion.2), kind=kOutput, calls=%fused_computation.7 | convolution fusion | flops 1078198272 | bytes 17301760 | tf_op jit(solution)/shard_map/bnrc,bncp->brp/dot_general | solution.py:41
  60.1 0.0 copy-start.2
  60.1 0.0 copy-done
  60.1 1.8 %fusion.10 = f32[256,2048]{1,0:T(8,128)} fusion(bf16[2048,128]{1,0:T(8,128)(2,1)S(1)} %bitcast.54, bf16[512,256]{1,0:T(8,128)(2,1)S(1)} %copy-done, s32[]{:T(128)S(6)} %select_n.15), kind=kOutput, calls=%fused_computation.11 | convolution fusion | flops 134217728 | bytes 2686980 | tf_op jit(solution)/shard_map/dot_general | solution.py:47
  61.9 0.0 reduce-scatter.2.cloned.1.call-update
  61.9 31.2 %reduce-scatter.2.cloned.1.call-done = f32[64,2048]{1,0:T(8,128)} async-done(((f32[256,2048]{1,0:T(8,128)}), f32[64,2048]{1,0:T(8,128)}) %reduce-scatter.2.cloned.1.call-update) | async-done | bytes 524304 | tf_op jit(solution)/shard_map/reduce_scatter | solution.py:46
  93.1 0.0 copy-start.1
  93.1 1.8 %fusion.26 = f32[64,64]{1,0:T(8,128)S(1)} fusion(f32[64,2048]{1,0:T(8,128)} %reduce-scatter.2.cloned.1.call-done), kind=kOutput, calls=%fused_computation.50 | convolution fusion | flops 100663296 | bytes 540672 | tf_op jit(solution)/shard_map/dot_general | solution.py:53
  94.9 0.0 copy-done.2
  94.9 0.1 copy.7
  95.0 5.8 %cholesky.74 = f32[64,64]{1,0:T(8,128)S(1)} custom-call(f32[64,64]{1,0:T(8,128)S(1)} %fusion.17), custom_call_target="Cholesky" | custom-call | tf_op jit(solution)/shard_map/jit(cholesky)/cholesky | solution.py:54
  100.9 0.6 compare_reduce_fusion.3
  101.5 0.7 select_select_fusion.3
  102.2 1.5 %collective-permute-start.4 = (f32[64,64]{1,0:T(8,128)S(1)}, f32[64,64]{1,0:T(8,128)S(1)}, u32[]{:S(2)}, u32[]{:S(2)}) collective-permute-start(f32[64,64]{1,0:T(8,128)S(1)} %select_select_fusion.3), channel_id=1, source_target_pairs={{0,4},{4,0},{8,12},{12,8},{16,20},{20,16},{24,28},{28,24},{1,5},{5... | collective-permute-start | bytes 49160 | tf_op jit(solution)/shard_map/ppermute | solution.py:20
  103.8 0.2 fusion.27
  103.9 2.2 %collective-permute-done.4 = f32[64,64]{1,0:T(8,128)S(1)} collective-permute-done((f32[64,64]{1,0:T(8,128)S(1)}, f32[64,64]{1,0:T(8,128)S(1)}, u32[]{:S(2)}, u32[]{:S(2)}) %collective-permute-start.4) | collective-permute-done | bytes 16416 | tf_op jit(solution)/shard_map/ppermute | solution.py:20
  106.2 0.2 convolution_add_fusion.2
  106.4 0.1 copy.10
  106.5 5.8 %cholesky.85 = f32[64,64]{1,0:T(8,128)S(1)} custom-call(f32[64,64]{1,0:T(8,128)S(1)} %fusion.16), custom_call_target="Cholesky" | custom-call | tf_op jit(solution)/shard_map/jit(cholesky)/cholesky | solution.py:60
  112.4 0.6 compare_reduce_fusion.2
  113.0 0.7 select_select_fusion.2
  113.7 1.6 %collective-permute-start.5 = (f32[64,64]{1,0:T(8,128)S(1)}, f32[64,64]{1,0:T(8,128)S(1)}, u32[]{:S(2)}, u32[]{:S(2)}) collective-permute-start(f32[64,64]{1,0:T(8,128)S(1)} %select_select_fusion.2), channel_id=1, source_target_pairs={{0,8},{4,12},{8,0},{12,4},{16,24},{20,28},{24,16},{28,20},{1,9},{5... | collective-permute-start | bytes 49160 | tf_op jit(solution)/shard_map/ppermute | solution.py:20
  115.2 0.2 fusion.28
  115.4 2.2 %collective-permute-done.5 = f32[64,64]{1,0:T(8,128)S(1)} collective-permute-done((f32[64,64]{1,0:T(8,128)S(1)}, f32[64,64]{1,0:T(8,128)S(1)}, u32[]{:S(2)}, u32[]{:S(2)}) %collective-permute-start.5) | collective-permute-done | bytes 16416 | tf_op jit(solution)/shard_map/ppermute | solution.py:20
  117.6 0.2 convolution_add_fusion.1
  117.8 0.1 copy.13
  117.9 5.8 %cholesky.96 = f32[64,64]{1,0:T(8,128)S(1)} custom-call(f32[64,64]{1,0:T(8,128)S(1)} %fusion.15), custom_call_target="Cholesky" | custom-call | tf_op jit(solution)/shard_map/jit(cholesky)/cholesky | solution.py:60
  123.8 0.6 compare_reduce_fusion.1
  124.4 0.7 select_select_fusion.1
  125.1 2.5 %collective-permute-start.6 = (f32[64,64]{1,0:T(8,128)S(1)}, f32[64,64]{1,0:T(8,128)S(1)}, u32[]{:S(2)}, u32[]{:S(2)}) collective-permute-start(f32[64,64]{1,0:T(8,128)S(1)} %select_select_fusion.1), channel_id=1, source_target_pairs={{0,16},{4,20},{8,24},{12,28},{16,0},{20,4},{24,8},{28,12},{1,17},{... | collective-permute-start | bytes 49160 | tf_op jit(solution)/shard_map/ppermute | solution.py:20
  127.6 0.2 fusion.29
  127.8 2.2 %collective-permute-done.6 = f32[64,64]{1,0:T(8,128)S(1)} collective-permute-done((f32[64,64]{1,0:T(8,128)S(1)}, f32[64,64]{1,0:T(8,128)S(1)}, u32[]{:S(2)}, u32[]{:S(2)}) %collective-permute-start.6) | collective-permute-done | bytes 16416 | tf_op jit(solution)/shard_map/ppermute | solution.py:20
  130.0 0.2 convolution_add_fusion
  130.2 0.1 copy.16
  130.3 5.8 %cholesky.107 = f32[64,64]{1,0:T(8,128)S(1)} custom-call(f32[64,64]{1,0:T(8,128)S(1)} %fusion.14), custom_call_target="Cholesky" | custom-call | tf_op jit(solution)/shard_map/jit(cholesky)/cholesky | solution.py:60
  136.2 0.6 compare_reduce_fusion
  136.8 0.7 fusion.12
  137.5 4.9 %custom-call.5 = f32[1,64,64]{1,2,0:T(8,128)S(1)} custom-call(f32[1,64,64]{2,1,0:T(8,128)S(1)} %fusion.12), custom_call_target="InvertDiagBlocksLowerTriangular" | custom-call | tf_op jit(solution)/shard_map/triangular_solve | solution.py:61
  142.4 0.0 copy-done.1
  142.4 1.4 convolution_multiply_fusion
  (9 shorter events, 0.2 us)
Async XLA Ops:
  7.2 52.9 %copy-start = (bf16[512,256]{1,0:T(8,128)(2,1)S(1)}, bf16[512,256]{1,0:T(8,128)(2,1)}, u32[]{:S(2)}) copy-start(bf16[512,256]{1,0:T(8,128)(2,1)} %param.10) | copy-start | bytes 786436
  7.2 85.9 %reduce-scatter.2.cloned.1.call-start = ((), (), s32[]{:S(2)}) async-start(), calls=%async_computation.1 | async-start | bytes 2621440 | tf_op jit(solution)/shard_map/reduce_scatter | solution.py:46
  7.2 16.6 %collective-permute-start = (bf16[16,128,128]{2,1,0:T(8,128)(2,1)}, bf16[16,128,128]{2,1,0:T(8,128)(2,1)}, u32[]{:S(2)}, u32[]{:S(2)}) collective-permute-start(bf16[16,128,128]{2,1,0:T(8,128)(2,1)} %bitcast.49), channel_id=1, source_target_pairs={{0,8},{4,12},{8,16},{12,20},{16,24},{20,28},{1,9},{5,13},{9,17},{1... | collective-permute-start | bytes 1572872 | tf_op jit(solution)/shard_map/ppermute | solution.py:14
  13.1 25.9 %collective-permute-start.1 = (bf16[16,128,128]{2,1,0:T(8,128)(2,1)}, bf16[16,128,128]{2,1,0:T(8,128)(2,1)}, u32[]{:S(2)}, u32[]{:S(2)}) collective-permute-start(bf16[16,128,128]{2,1,0:T(8,128)(2,1)} %bitcast.50), channel_id=1, source_target_pairs={{0,4},{4,8},{8,12},{12,16},{16,20},{20,24},{24,28},{1,5},{5,9},{9,... | collective-permute-start | bytes 1572872 | tf_op jit(solution)/shard_map/ppermute | solution.py:14
  17.3 23.9 %collective-permute-start.2 = (bf16[16,128,128]{2,1,0:T(8,128)(2,1)}, bf16[16,128,128]{2,1,0:T(8,128)(2,1)}, u32[]{:S(2)}, u32[]{:S(2)}) collective-permute-start(bf16[16,128,128]{2,1,0:T(8,128)(2,1)} %bitcast.51), channel_id=1, source_target_pairs={{4,0},{8,4},{12,8},{16,12},{20,16},{24,20},{28,24},{5,1},{9,5},{13... | collective-permute-start | bytes 1572872 | tf_op jit(solution)/shard_map/ppermute | solution.py:14
  18.6 24.6 %collective-permute-start.3 = (bf16[16,128,128]{2,1,0:T(8,128)(2,1)}, bf16[16,128,128]{2,1,0:T(8,128)(2,1)S(1)}, u32[]{:S(2)}, u32[]{:S(2)}) collective-permute-start(bf16[16,128,128]{2,1,0:T(8,128)(2,1)} %bitcast.52), channel_id=1, source_target_pairs={{8,0},{12,4},{16,8},{20,12},{24,16},{28,20},{9,1},{13,5},{17,9},{2... | collective-permute-start | bytes 1572872 | tf_op jit(solution)/shard_map/ppermute | solution.py:14
  60.1 34.9 %copy-start.2 = (bf16[16,128,128]{1,2,0:T(8,128)(2,1)}, bf16[16,128,128]{1,2,0:T(8,128)(2,1)S(1)}, u32[]{:S(2)}) copy-start(bf16[16,128,128]{1,2,0:T(8,128)(2,1)S(1)} %fusion.7) | copy-start | bytes 1572868
  93.1 49.3 %copy-start.1 = (f32[64,2048]{1,0:T(8,128)S(1)}, f32[64,2048]{1,0:T(8,128)}, u32[]{:S(2)}) copy-start(f32[64,2048]{1,0:T(8,128)} %reduce-scatter.2.cloned.1.call-done) | copy-start | bytes 1572868
  102.2 4.0 %collective-permute-start.4 = (f32[64,64]{1,0:T(8,128)S(1)}, f32[64,64]{1,0:T(8,128)S(1)}, u32[]{:S(2)}, u32[]{:S(2)}) collective-permute-start(f32[64,64]{1,0:T(8,128)S(1)} %select_select_fusion.3), channel_id=1, source_target_pairs={{0,4},{4,0},{8,12},{12,8},{16,20},{20,16},{24,28},{28,24},{1,5},{5... | collective-permute-start | bytes 49160 | tf_op jit(solution)/shard_map/ppermute | solution.py:20
  113.7 4.0 %collective-permute-start.5 = (f32[64,64]{1,0:T(8,128)S(1)}, f32[64,64]{1,0:T(8,128)S(1)}, u32[]{:S(2)}, u32[]{:S(2)}) collective-permute-start(f32[64,64]{1,0:T(8,128)S(1)} %select_select_fusion.2), channel_id=1, source_target_pairs={{0,8},{4,12},{8,0},{12,4},{16,24},{20,28},{24,16},{28,20},{1,9},{5... | collective-permute-start | bytes 49160 | tf_op jit(solution)/shard_map/ppermute | solution.py:20
  125.1 4.9 %collective-permute-start.6 = (f32[64,64]{1,0:T(8,128)S(1)}, f32[64,64]{1,0:T(8,128)S(1)}, u32[]{:S(2)}, u32[]{:S(2)}) collective-permute-start(f32[64,64]{1,0:T(8,128)S(1)} %select_select_fusion.1), channel_id=1, source_target_pairs={{0,16},{4,20},{8,24},{12,28},{16,0},{20,4},{24,8},{28,12},{1,17},{... | collective-permute-start | bytes 49160 | tf_op jit(solution)/shard_map/ppermute | solution.py:20
Sparse Core Ops, SparseCore 0:
  62.0 30.9 reduce-scatter.1
where the time goes:
time: 151 us
  waiting for transfers between devices  55.1 us (36%)
  other arithmetic  35.1 us (23%)
  starting transfers between devices  18.3 us (12%)
  matrix products  14.3 us (9%)
  between operations  14.3 us (9%)
  local copies, waits for them, and re-layouts  13.5 us (9%)
    reduce_scatter x1, waiting for transfers between devices, shards(): lax.psum_scatter(lax.dot_general(psi_rows, sample, contract, preferred_el...  31.2 us
    another operation x9, other arithmetic, shards(): lower = jnp.linalg.cholesky(stacked)  19.6 us
    ppermute x4, waiting for transfers between devices, passed_along(): lax.ppermute(value, axis, [(source, source + steps) for source in range(i...  17.3 us
    ppermute x4, starting transfers between devices, passed_along(): lax.ppermute(value, axis, [(source, source + steps) for source in range(i...  12.7 us
    gather x1, local copies, waits for them, and re-layouts, shards(): picked = window[local_ids]  8.62 us
    dot_general x1, matrix products, shards(): jnp.einsum('bnrc,bncp->brp', near_field, picked, preferred_element_type=j...  8.17 us
    ppermute x3, waiting for transfers between devices, partner_2(): return lax.ppermute(value, axis, pairs)  6.68 us
    another operation x3, other arithmetic, shards(): lower = jnp.linalg.cholesky(gram_local)  6.52 us
  transfers between devices with their start and end apart: 8, of which 7 were waited for; matrix products, arithmetic and copies ran while one was open for 4% of the time, Pallas kernels for 0%

commit v1 on v0

v1 whole, which is shorter than its diff:
```python
import functools
import math

import jax
import jax.numpy as jnp
from jax import lax
from jax.experimental import pallas as pl
from jax.experimental.pallas import tpu as pltpu
from jax.sharding import PartitionSpec as P

REACH = 2
MESH = pl.DeviceIdType.MESH
F32 = jnp.float32
BF16 = jnp.bfloat16
CHUNKS = 4
NT = (((1,), (1,)), ((), ()))
NN = (((1,), (0,)), ((), ()))
HIGHEST = lax.Precision.HIGHEST


def kernel(
    patches, total_rows, probe, nf, ids, counts, psi, sample_out, basis_out,
    win, nfv, idx, psiv, psit, samp, keep, send, crecv, fac, xsend, xrecv, gsend, grecv, bas,
    hs, hr, ls, nfs, sos, cs, cr, xs, xr, gs, gr, bos,
):
    blk_dev, slots, blk, width = nf.shape[0], nf.shape[1], nf.shape[2], probe.shape[2]
    half = blk_dev // 2
    sketch = psi.shape[1]
    rank = sketch // 4
    per = blk_dev // CHUNKS
    cw = per * blk
    levels = patches.bit_length() - 1

    p = lax.axis_index("patch")
    me = lax.axis_index("probe")
    s = 1 - 2 * (p % 2)
    near = p + s
    ahead = p + 2 * s
    behind = p - 2 * s
    has_ahead = jnp.logical_and(ahead >= 0, ahead < patches)
    has_behind = jnp.logical_and(behind >= 0, behind < patches)
    core = me + 1 - 2 * (me % 2)
    side = me + 2 - 4 * (me // 2)

    def flip(level):
        bit = 2**level
        return p + bit - 2 * bit * ((p // bit) % 2)

    barrier = pltpu.get_barrier_semaphore()

    def greet(where):
        pl.semaphore_signal(barrier, inc=1, device_id=where, device_id_type=MESH)

    greet({"patch": near})
    greet({"probe": core})
    greet({"probe": side})
    for level in range(2, levels):
        greet({"patch": flip(level)})

    @pl.when(has_ahead)
    def _():
        greet({"patch": ahead})

    @pl.when(has_behind)
    def _():
        greet({"patch": behind})

    own_copy = pltpu.make_async_copy(probe, win.at[pl.ds(0, blk_dev)], ls.at[0])
    own_copy.start()
    psi_copy = pltpu.make_async_copy(
        psi.at[pl.ds(pl.multiple_of(me * width, width), width)], psiv, ls.at[1]
    )
    psi_copy.start()

    peers = 3 + max(levels - 2, 0) + has_ahead.astype(jnp.int32) + has_behind.astype(jnp.int32)
    pl.semaphore_wait(barrier, peers)

    def halo(k, src, slot, start, count, target):
        return pltpu.make_async_remote_copy(
            src_ref=src, dst_ref=win.at[pl.ds(slot * blk_dev + start, count)],
            send_sem=hs.at[k], recv_sem=hr.at[k], device_id={"patch": target}, device_id_type=MESH,
        )

    first, second = probe.at[pl.ds(0, half)], probe.at[pl.ds(half, half)]
    near_b = halo(0, second, 1, half, half, near)
    near_a = halo(1, first, 1, 0, half, near)
    behind_a = halo(2, first, 2, 0, half, behind)
    behind_b = halo(3, second, 2, half, half, behind)
    ahead_a = halo(4, first, 3, 0, half, ahead)
    ahead_b = halo(5, second, 3, half, half, ahead)
    relay_a = halo(6, win.at[pl.ds(2 * blk_dev, half)], 4, 0, half, near)
    relay_b = halo(7, win.at[pl.ds(blk_dev + half, half)], 4, half, half, ahead)

    near_b.start()

    @pl.when(has_behind)
    def _():
        behind_a.start()

    @pl.when(has_ahead)
    def _():
        ahead_a.start()

    near_a.start()

    @pl.when(has_behind)
    def _():
        behind_b.start()

    @pl.when(has_ahead)
    def _():
        ahead_b.start()

    nf_copies = []
    for c in range(CHUNKS):
        rows = pl.ds(c * per, per)
        copy = pltpu.make_async_copy(nf.at[rows], nfv.at[rows], nfs.at[c])
        copy.start()
        nf_copies.append(copy)

    zero_block = (2 * REACH + 1) * blk_dev
    win[zero_block] = jnp.zeros((blk, width), BF16)

    @pl.loop(0, blk_dev)
    def _(b):
        live = counts[b]
        for n in range(slots):
            column = ids[b, n]
            turn = (column // blk_dev - p) * s
            slot = jnp.where(turn < 0, turn + 2 * REACH + 1, turn)
            place = slot * blk_dev + column % blk_dev
            idx[b, n] = jnp.where(n < live, place, zero_block)

    psi_copy.wait()
    psit[...] = psiv[...].astype(F32).T.astype(BF16).reshape(4, rank, width)
    other = side + 1 - 2 * (side % 2)
    psiq = jnp.concatenate([psit[me], psit[side], psit[core], psit[other]], 0)

    near_b.wait_recv()

    @pl.when(has_ahead)
    def _():
        relay_b.start()
        behind_a.wait_recv()
        relay_a.start()
        behind_b.wait_recv()

    near_a.wait_recv()

    @pl.when(has_behind)
    def _():
        ahead_a.wait_recv()
        ahead_b.wait_recv()
        relay_a.wait_recv()
        relay_b.wait_recv()

    own_copy.wait()

    def core_copy(c):
        return pltpu.make_async_remote_copy(
            src_ref=send.at[c], dst_ref=crecv.at[c], send_sem=cs.at[c], recv_sem=cr.at[c],
            device_id={"probe": core}, device_id_type=MESH,
        )

    def side_copy(c):
        return pltpu.make_async_remote_copy(
            src_ref=xsend.at[c], dst_ref=xrecv.at[c], send_sem=xs.at[c], recv_sem=xr.at[c],
            device_id={"probe": side}, device_id_type=MESH,
        )

    def pass_on(c):
        core_copy(c).wait_recv()
        both = keep[c] + crecv[c]
        fac[c] = both[:rank]
        xsend[c] = both[rank:].astype(BF16)
        side_copy(c).start()

    sample_copies = []
    for c in range(CHUNKS):
        nf_copies[c].wait()

        @pl.loop(c * per, (c + 1) * per)
        def _(b):
            picked = jnp.concatenate([win[idx[b, n]] for n in range(slots)], 0)
            blocks = jnp.concatenate([nfv[b, n] for n in range(slots)], 1)
            samp[b] = lax.dot_general(blocks, picked, NN, preferred_element_type=F32).astype(BF16)

        rows = pl.ds(c * per, per)
        copy = pltpu.make_async_copy(samp.at[rows], sample_out.at[rows], sos.at[c])
        copy.start()
        sample_copies.append(copy)
        part = lax.dot_general(
            psiq, samp[rows].reshape(cw, width), NT, preferred_element_type=F32
        )
        keep[c] = part[: 2 * rank]
        send[c] = part[2 * rank :]
        core_copy(c).start()
        if c > 0:
            pass_on(c - 1)
    pass_on(CHUNKS - 1)

    gram = jnp.zeros((rank, 2 * rank), F32)
    for c in range(CHUNKS):
        side_copy(c).wait_recv()
        factor = fac[c] + xrecv[c].astype(F32)
        fac[c] = factor
        twice = jnp.concatenate([factor, factor], 0)
        gram += lax.dot_general(factor, twice, NT, precision=HIGHEST, preferred_element_type=F32)

    lane = lax.broadcasted_iota(jnp.int32, (rank // 2, 2 * rank), 1)
    packed = jnp.where(lane < rank, gram[: rank // 2], gram[rank // 2 :])

    def gram_copy(level):
        return pltpu.make_async_remote_copy(
            src_ref=gsend.at[level], dst_ref=grecv.at[level], send_sem=gs.at[level],
            recv_sem=gr.at[level], device_id={"patch": flip(level)}, device_id_type=MESH,
        )

    for level in range(levels):
        gsend[level] = packed
        gram_copy(level).start()
        gram_copy(level).wait_recv()
        packed = packed + grecv[level]

    lane = lax.broadcasted_iota(jnp.int32, (rank, 2 * rank), 1)
    row = lax.broadcasted_iota(jnp.int32, (rank, 2 * rank), 0)
    work = jnp.concatenate([pltpu.roll(packed, rank, 1), packed], 0)
    work = jnp.where(lane < rank, jnp.where(lane == row, 1.0, 0.0), work)
    for j in range(rank - 1):
        column = jnp.broadcast_to(work[:, rank + j : rank + j + 1], work.shape)
        pivot_row = work[j : j + 1, :]
        ratio = pivot_row / column[j : j + 1, :]
        work = jnp.where(row > j, work - column * ratio, work)
    pivots = jnp.sum(jnp.where(lane == row + rank, work, 0.0), axis=1, keepdims=True)
    inverse = work[:, :rank] * (lax.rsqrt(pivots) * math.sqrt(total_rows))

    basis_copies = []
    for c in range(CHUNKS):
        columns = pl.ds(c * cw, cw)
        bas[:, columns] = lax.dot_general(
            inverse, fac[c], NN, precision=HIGHEST, preferred_element_type=F32
        )
        copy = pltpu.make_async_copy(bas.at[:, columns], basis_out.at[:, columns], bos.at[c])
        copy.start()
        basis_copies.append(copy)

    near_b.wait_send()
    near_a.wait_send()

    @pl.when(has_behind)
    def _():
        behind_a.wait_send()
        behind_b.wait_send()

    @pl.when(has_ahead)
    def _():
        ahead_a.wait_send()
        ahead_b.wait_send()
        relay_a.wait_send()
        relay_b.wait_send()

    for c in range(CHUNKS):
        core_copy(c).wait_send()
        side_copy(c).wait_send()
        sample_copies[c].wait()
        basis_copies[c].wait()
    for level in range(levels):
        gram_copy(level).wait_send()


def shards(probe_columns, near_field, column_ids, block_counts, sketch_matrix):
    blk_dev, slots, blk, _ = near_field.shape
    rows, width = probe_columns.shape
    sketch = sketch_matrix.shape[1]
    patches = lax.axis_size("patch")
    rank = sketch // lax.axis_size("probe")
    cw = rows // CHUNKS
    levels = patches.bit_length() - 1
    anywhere = pl.BlockSpec(memory_space=pl.ANY)
    scalars = pl.BlockSpec(memory_space=pltpu.SMEM)
    dma = pltpu.SemaphoreType.DMA
    sample, basis = pl.pallas_call(
        functools.partial(kernel, patches, rows * patches),
        out_shape=[
            jax.ShapeDtypeStruct((blk_dev, blk, width), BF16),
            jax.ShapeDtypeStruct((rank, rows), F32),
        ],
        in_specs=[anywhere, anywhere, scalars, scalars, anywhere],
        out_specs=[anywhere, anywhere],
        scratch_shapes=[
            pltpu.VMEM(((2 * REACH + 1) * blk_dev + 1, blk, width), BF16),
            pltpu.VMEM(near_field.shape, BF16),
            pltpu.SMEM((blk_dev, slots), jnp.int32),
            pltpu.VMEM((width, sketch), BF16),
            pltpu.VMEM((4, rank, width), BF16),
            pltpu.VMEM((blk_dev, blk, width), BF16),
            pltpu.VMEM((CHUNKS, 2 * rank, cw), F32),
            pltpu.VMEM((CHUNKS, 2 * rank, cw), F32),
            pltpu.VMEM((CHUNKS, 2 * rank, cw), F32),
            pltpu.VMEM((CHUNKS, rank, cw), F32),
            pltpu.VMEM((CHUNKS, rank, cw), BF16),
            pltpu.VMEM((CHUNKS, rank, cw), BF16),
            pltpu.VMEM((levels, rank // 2, 2 * rank), F32),
            pltpu.VMEM((levels, rank // 2, 2 * rank), F32),
            pltpu.VMEM((rank, rows), F32),
            dma((8,)), dma((8,)), dma((2,)), dma((CHUNKS,)), dma((CHUNKS,)),
            dma((CHUNKS,)), dma((CHUNKS,)), dma((CHUNKS,)), dma((CHUNKS,)),
            dma((levels,)), dma((levels,)), dma((CHUNKS,)),
        ],
        compiler_params=pltpu.CompilerParams(
            collective_id=0, has_side_effects=True, vmem_limit_bytes=48 * 2**20
        ),
    )(
        probe_columns.reshape(blk_dev, blk, width), near_field, column_ids, block_counts,
        sketch_matrix,
    )
    return (sample.reshape(rows, width), basis)


def solution(mesh):
    placed = (P("patch", "probe"), P("patch", None, None, None), P("patch", None), P("patch"), P())
    return jax.shard_map(
        shards,
        mesh=mesh,
        in_specs=placed,
        out_specs=(P("patch", "probe"), P("probe", "patch")),
        check_vma=False,
    )
```

time: 151 us -> 55.7 us (0.37)
  waiting for transfers between devices: 55.1 us -> 0 us
  Pallas kernels: 0 us -> 49.2 us
  other arithmetic: 35.1 us -> 0 us
  starting transfers between devices: 18.3 us -> 0 us
  matrix products: 14.3 us -> 0 us
  between operations: 14.3 us -> 0.65 us
  local copies, waits for them, and re-layouts: 13.5 us -> 4.92 us
    pallas_call x0 -> x1, Pallas kernels: none -> 49.2 us  [shards(): pl.pallas_call(functools.partial(kernel, patches, rows * patches), out_sh...]
    another operation x14 -> x0, other arithmetic: 31.6 us -> none  [the longest x9 19.6 us: shards(): lower = jnp.linalg.cholesky(stacked)]
    reduce_scatter x1 -> x0, waiting for transfers between devices: 31.2 us -> none  [shards(): lax.psum_scatter(lax.dot_general(psi_rows, sample, contract, preferred_el...]
    ppermute x7 -> x0, waiting for transfers between devices: 24 us -> none  [the longest x4 17.3 us: passed_along(): lax.ppermute(value, axis, [(source, source + steps) for source in range(i...]
    ppermute x7 -> x0, starting transfers between devices: 18.2 us -> none  [the longest x4 12.7 us: passed_along(): lax.ppermute(value, axis, [(source, source + steps) for source in range(i...]
    dot_general x9 -> x0, matrix products: 12.9 us -> none  [the longest x1 8.17 us: shards(): jnp.einsum('bnrc,bncp->brp', near_field, picked, preferred_element_type=j...]
    gather x1 -> x0, local copies, waits for them, and re-layouts: 8.62 us -> none  [shards(): picked = window[local_ids]]
    select_n x4 -> x0, other arithmetic: 2.66 us -> none  [the longest x2 1.3 us: shards(): lower = jnp.linalg.cholesky(stacked)]
  transfers between devices with their start and end apart: 8 -> 0, of which waited for: 7 -> 0; matrix products, arithmetic and copies ran while one was open for 4% -> 0% of each run, Pallas kernels for 0% -> 0%
where the time goes in v1:
time: 55.7 us; the launch traced here: 54.7 us
  Pallas kernels  49.2 us (88%)
  local copies, waits for them, and re-layouts  4.92 us (9%)
  between operations  0.65 us (1%)
    pallas_call x1, Pallas kernels, shards(): pl.pallas_call(functools.partial(kernel, patches, rows * patches), out_sh...  49.2 us
    unnamed x10, local copies, waits for them, and re-layouts  4.92 us

profile of v1, /device:TPU:0, one launch (start us, length us, event | category | flops | bytes accessed | tf_op | source)
XLA Modules:
  0.0 54.7 jit_solution(10837309138555324016)
XLA Ops:
  0.6 0.0 copy-start
  0.6 1.0 %copy-done = bf16[2048,128]{1,0:T(8,128)(2,1)S(1)} copy-done((bf16[2048,128]{1,0:T(8,128)(2,1)S(1)}, bf16[2048,128]{1,0:T(8,128)(2,1)}, u32[]{:S(2)}) %copy-start) | copy-done | bytes 524312
  1.7 0.0 copy-start.1
  1.7 0.9 %copy-done.1 = bf16[512,256]{1,0:T(8,128)(2,1)S(1)} copy-done((bf16[512,256]{1,0:T(8,128)(2,1)S(1)}, bf16[512,256]{1,0:T(8,128)(2,1)}, u32[]{:S(2)}) %copy-start.1) | copy-done | bytes 262168
  2.6 0.0 copy-start.2
  2.6 0.7 %copy-done.2 = s32[16,16]{1,0:T(8,128)S(1)} copy-done((s32[16,16]{1,0:T(8,128)S(1)}, s32[16,16]{1,0:T(8,128)}, u32[]{:S(2)}) %copy-start.2) | copy-done | bytes 1048
  3.3 0.0 copy-start.3
  3.3 0.7 %copy-done.3 = s32[16]{0:T(128)S(1)} copy-done((s32[16]{0:T(128)S(1)}, s32[16]{0:T(128)}, u32[]{:S(2)}) %copy-start.3) | copy-done | bytes 88
  4.0 49.2 %shard_map.68 = (bf16[16,128,128]{2,1,0:T(8,128)(2,1)S(1)}, f32[64,2048]{1,0:T(8,128)S(1)}) custom-call(bf16[16,128,128]{2,1,0:T(8,128)(2,1)S(1)} %bitcast.3, bf16[16,16,128,128]{3,2,1,0:T(8,128)(2,1)} %nf.1, s32[16,16]{1,0:T(8,128)S(1)} %copy-done.2, s32[16]{0:T(128)S(1)} %copy-done.3, bf16[512,256]{1,0:T(8,128)(2,1)S(1)} %copy-done.1), custom_call_target="tpu_custom_call" | custom-call | tf_op jit(solution)/shard_map/pallas_call | solution.py:282
  53.1 0.8 %copy.9 = bf16[2048,128]{1,0:T(8,128)(2,1)} copy(bf16[2048,128]{1,0:T(8,128)(2,1)S(1)} %bitcast.2) | data formatting | bytes 1048576
  53.9 0.8 %copy.10 = f32[64,2048]{1,0:T(8,128)} copy(f32[64,2048]{1,0:T(8,128)S(1)} %get-tuple-element.9) | data formatting | bytes 1048576
Async XLA Ops:
  0.6 1.0 %copy-start = (bf16[2048,128]{1,0:T(8,128)(2,1)S(1)}, bf16[2048,128]{1,0:T(8,128)(2,1)}, u32[]{:S(2)}) copy-start(bf16[2048,128]{1,0:T(8,128)(2,1)} %param.5) | copy-start | bytes 1572868
  1.7 0.9 %copy-start.1 = (bf16[512,256]{1,0:T(8,128)(2,1)S(1)}, bf16[512,256]{1,0:T(8,128)(2,1)}, u32[]{:S(2)}) copy-start(bf16[512,256]{1,0:T(8,128)(2,1)} %psi.1) | copy-start | bytes 786436
  2.6 0.7 %copy-start.2 = (s32[16,16]{1,0:T(8,128)S(1)}, s32[16,16]{1,0:T(8,128)}, u32[]{:S(2)}) copy-start(s32[16,16]{1,0:T(8,128)} %ids.1) | copy-start | bytes 3076
  3.3 0.7 %copy-start.3 = (s32[16]{0:T(128)S(1)}, s32[16]{0:T(128)}, u32[]{:S(2)}) copy-start(s32[16]{0:T(128)} %counts.1) | copy-start | bytes 196

commit v2 on v1

--- a/solution.py
+++ b/solution.py
@@ -15,12 +15,50 @@
 CHUNKS = 4
 NT = (((1,), (1,)), ((), ()))
 NN = (((1,), (0,)), ((), ()))
-HIGHEST = lax.Precision.HIGHEST
+ROW_TILE = 8
+
+
+def exchange_plan(patches):
+    levels = patches.bit_length() - 1
+    return [
+        [digit << low for digit in range(1, 2 ** min(3, levels - low))]
+        for low in range(0, levels, 3)
+    ]
+
+
+def eliminate(work, rank):
+    tile = ROW_TILE
+    shape = (tile, work.shape[1])
+    tiles = [work[i : i + tile] for i in range(0, rank, tile)]
+    row = lax.broadcasted_iota(jnp.int32, shape, 0)
+    lane = lax.broadcasted_iota(jnp.int32, shape, 1)
+    for t in range(len(tiles)):
+        live = range(t, len(tiles))
+        columns = [
+            {i: jnp.broadcast_to(tiles[i][:, rank + t * tile + k : rank + t * tile + k + 1], shape) for i in live}
+            for k in range(tile)
+        ]
+        for k in range(tile):
+            scale = 1.0 / columns[k][t][k : k + 1, :]
+            ratio = {i: columns[k][i] * scale for i in live}
+            ratio[t] = jnp.where(row > k, ratio[t], 0.0)
+            for later in columns[k + 1 :]:
+                pivot = later[t][k : k + 1, :]
+                for i in live:
+                    later[i] = later[i] - ratio[i] * pivot
+            pivot = tiles[t][k : k + 1, :]
+            for i in live:
+                tiles[i] = tiles[i] - ratio[i] * pivot
+    diagonal = [
+        jnp.sum(jnp.where(lane == row + rank + i * tile, part, 0.0), axis=1, keepdims=True)
+        for i, part in enumerate(tiles)
+    ]
+    return jnp.concatenate(tiles, 0), jnp.concatenate(diagonal, 0)
 
 
 def kernel(
-    patches, total_rows, probe, nf, ids, counts, psi, sample_out, basis_out,
-    win, nfv, idx, psiv, psit, samp, keep, send, crecv, fac, xsend, xrecv, gsend, grecv, bas,
+    patches, total_rows, probe, nf, ids_in, counts_in, psi, sample_out, basis_out,
+    win, nfv, ids, counts, idx, psiv, psit, samp, keep, send, crecv, fac, xsend, xrecv, split, gsend, grecv, bas,
     hs, hr, ls, nfs, sos, cs, cr, xs, xr, gs, gr, bos,
 ):
     blk_dev, slots, blk, width = nf.shape[0], nf.shape[1], nf.shape[2], probe.shape[2]
@@ -42,26 +80,34 @@
     core = me + 1 - 2 * (me % 2)
     side = me + 2 - 4 * (me // 2)
 
-    def flip(level):
-        bit = 2**level
-        return p + bit - 2 * bit * ((p // bit) % 2)
+    def other_patch(mask):
+        place = p
+        for bit in (2**level for level in range(levels)):
+            if mask & bit:
+                place = place + bit - 2 * bit * ((p // bit) % 2)
+        return place
+
+    peers = exchange_plan(patches)
+    group = peers[0][-1] + 1
 
     barrier = pltpu.get_barrier_semaphore()
 
     def greet(where):
         pl.semaphore_signal(barrier, inc=1, device_id=where, device_id_type=MESH)
 
-    greet({"patch": near})
+    ahead_out = jnp.logical_and(has_ahead, ahead // group != p // group)
+    behind_out = jnp.logical_and(has_behind, behind // group != p // group)
     greet({"probe": core})
     greet({"probe": side})
-    for level in range(2, levels):
-        greet({"patch": flip(level)})
-
-    @pl.when(has_ahead)
+    for stage in peers:
+        for mask in stage:
+            greet({"patch": other_patch(mask)})
+
+    @pl.when(ahead_out)
     def _():
         greet({"patch": ahead})
 
-    @pl.when(has_behind)
+    @pl.when(behind_out)
     def _():
         greet({"patch": behind})
 
@@ -71,9 +117,13 @@
         psi.at[pl.ds(pl.multiple_of(me * width, width), width)], psiv, ls.at[1]
     )
     psi_copy.start()
-
-    peers = 3 + max(levels - 2, 0) + has_ahead.astype(jnp.int32) + has_behind.astype(jnp.int32)
-    pl.semaphore_wait(barrier, peers)
+    ids_copy = pltpu.make_async_copy(ids_in, ids, ls.at[2])
+    ids_copy.start()
+    counts_copy = pltpu.make_async_copy(counts_in, counts, ls.at[3])
+    counts_copy.start()
+
+    greeted = 2 + sum(len(stage) for stage in peers)
+    pl.semaphore_wait(barrier, greeted + ahead_out.astype(jnp.int32) + behind_out.astype(jnp.int32))
 
     def halo(k, src, slot, start, count, target):
         return pltpu.make_async_remote_copy(
@@ -121,6 +171,9 @@
     zero_block = (2 * REACH + 1) * blk_dev
     win[zero_block] = jnp.zeros((blk, width), BF16)
 
+    ids_copy.wait()
+    counts_copy.wait()
+
     @pl.loop(0, blk_dev)
     def _(b):
         live = counts[b]
@@ -203,42 +256,51 @@
     for c in range(CHUNKS):
         side_copy(c).wait_recv()
         factor = fac[c] + xrecv[c].astype(F32)
-        fac[c] = factor
-        twice = jnp.concatenate([factor, factor], 0)
-        gram += lax.dot_general(factor, twice, NT, precision=HIGHEST, preferred_element_type=F32)
+        high = factor.astype(BF16)
+        low = (factor - high.astype(F32)).astype(BF16)
+        split[c] = jnp.concatenate([high, low, high], 0)
+        twice_high = jnp.concatenate([high, high], 0)
+        twice_low = jnp.concatenate([low, low], 0)
+        both = lax.dot_general(split[c, : 2 * rank], twice_high, NT, preferred_element_type=F32)
+        cross = lax.dot_general(high, twice_low, NT, preferred_element_type=F32)
+        gram += both[:rank] + (both[rank:] + cross)
 
     lane = lax.broadcasted_iota(jnp.int32, (rank // 2, 2 * rank), 1)
     packed = jnp.where(lane < rank, gram[: rank // 2], gram[rank // 2 :])
 
-    def gram_copy(level):
-        return pltpu.make_async_remote_copy(
-            src_ref=gsend.at[level], dst_ref=grecv.at[level], send_sem=gs.at[level],
-            recv_sem=gr.at[level], device_id={"patch": flip(level)}, device_id_type=MESH,
-        )
-
-    for level in range(levels):
-        gsend[level] = packed
-        gram_copy(level).start()
-        gram_copy(level).wait_recv()
-        packed = packed + grecv[level]
+    gram_copies = []
+    place = 0
+    for number, stage in enumerate(peers):
+        gsend[number] = packed
+        copies = []
+        for mask in stage:
+            copy = pltpu.make_async_remote_copy(
+                src_ref=gsend.at[number], dst_ref=grecv.at[place], send_sem=gs.at[place],
+                recv_sem=gr.at[place], device_id={"patch": other_patch(mask)}, device_id_type=MESH,
+            )
+            copy.start()
+            copies.append((copy, place))
+            place += 1
+        for copy, slot in copies:
+            copy.wait_recv()
+            packed = packed + grecv[slot]
+        gram_copies += copies
 
     lane = lax.broadcasted_iota(jnp.int32, (rank, 2 * rank), 1)
     row = lax.broadcasted_iota(jnp.int32, (rank, 2 * rank), 0)
     work = jnp.concatenate([pltpu.roll(packed, rank, 1), packed], 0)
     work = jnp.where(lane < rank, jnp.where(lane == row, 1.0, 0.0), work)
-    for j in range(rank - 1):
-        column = jnp.broadcast_to(work[:, rank + j : rank + j + 1], work.shape)
-        pivot_row = work[j : j + 1, :]
-        ratio = pivot_row / column[j : j + 1, :]
-        work = jnp.where(row > j, work - column * ratio, work)
-    pivots = jnp.sum(jnp.where(lane == row + rank, work, 0.0), axis=1, keepdims=True)
+    work, pivots = eliminate(work, rank)
     inverse = work[:, :rank] * (lax.rsqrt(pivots) * math.sqrt(total_rows))
+    inverse_high = inverse.astype(BF16)
+    inverse_low = (inverse - inverse_high.astype(F32)).astype(BF16)
+    inverse = jnp.concatenate([inverse_high, inverse_high, inverse_low], 1)
 
     basis_copies = []
     for c in range(CHUNKS):
         columns = pl.ds(c * cw, cw)
         bas[:, columns] = lax.dot_general(
-            inverse, fac[c], NN, precision=HIGHEST, preferred_element_type=F32
+            inverse, split[c], NN, preferred_element_type=F32
         )
         copy = pltpu.make_async_copy(bas.at[:, columns], basis_out.at[:, columns], bos.at[c])
         copy.start()
@@ -264,8 +326,8 @@
         side_copy(c).wait_send()
         sample_copies[c].wait()
         basis_copies[c].wait()
-    for level in range(levels):
-        gram_copy(level).wait_send()
+    for copy, _ in gram_copies:
+        copy.wait_send()
 
 
 def shards(probe_columns, near_field, column_ids, block_counts, sketch_matrix):
@@ -275,9 +337,9 @@
     patches = lax.axis_size("patch")
     rank = sketch // lax.axis_size("probe")
     cw = rows // CHUNKS
-    levels = patches.bit_length() - 1
-    anywhere = pl.BlockSpec(memory_space=pl.ANY)
-    scalars = pl.BlockSpec(memory_space=pltpu.SMEM)
+    plan = exchange_plan(patches)
+    sends = sum(len(stage) for stage in plan)
+    anywhere = pl.BlockSpec(memory_space=pltpu.HBM)
     dma = pltpu.SemaphoreType.DMA
     sample, basis = pl.pallas_call(
         functools.partial(kernel, patches, rows * patches),
@@ -285,11 +347,13 @@
             jax.ShapeDtypeStruct((blk_dev, blk, width), BF16),
             jax.ShapeDtypeStruct((rank, rows), F32),
         ],
-        in_specs=[anywhere, anywhere, scalars, scalars, anywhere],
+        in_specs=[anywhere] * 5,
         out_specs=[anywhere, anywhere],
         scratch_shapes=[
             pltpu.VMEM(((2 * REACH + 1) * blk_dev + 1, blk, width), BF16),
             pltpu.VMEM(near_field.shape, BF16),
+            pltpu.SMEM((blk_dev, slots), jnp.int32),
+            pltpu.SMEM((blk_dev,), jnp.int32),
             pltpu.SMEM((blk_dev, slots), jnp.int32),
             pltpu.VMEM((width, sketch), BF16),
             pltpu.VMEM((4, rank, width), BF16),
@@ -300,15 +364,16 @@
             pltpu.VMEM((CHUNKS, rank, cw), F32),
             pltpu.VMEM((CHUNKS, rank, cw), BF16),
             pltpu.VMEM((CHUNKS, rank, cw), BF16),
-            pltpu.VMEM((levels, rank // 2, 2 * rank), F32),
-            pltpu.VMEM((levels, rank // 2, 2 * rank), F32),
+            pltpu.VMEM((CHUNKS, 3 * rank, cw), BF16),
+            pltpu.VMEM((len(plan), rank // 2, 2 * rank), F32),
+            pltpu.VMEM((sends, rank // 2, 2 * rank), F32),
             pltpu.VMEM((rank, rows), F32),
-            dma((8,)), dma((8,)), dma((2,)), dma((CHUNKS,)), dma((CHUNKS,)),
+            dma((8,)), dma((8,)), dma((4,)), dma((CHUNKS,)), dma((CHUNKS,)),
             dma((CHUNKS,)), dma((CHUNKS,)), dma((CHUNKS,)), dma((CHUNKS,)),
-            dma((levels,)), dma((levels,)), dma((CHUNKS,)),
+            dma((sends,)), dma((sends,)), dma((CHUNKS,)),
         ],
         compiler_params=pltpu.CompilerParams(
-            collective_id=0, has_side_effects=True, vmem_limit_bytes=48 * 2**20
+            collective_id=0, has_side_effects=True, vmem_limit_bytes=64 * 2**20
         ),
     )(
         probe_columns.reshape(blk_dev, blk, width), near_field, column_ids, block_counts,

time: 55.7 us -> 47.8 us (0.86); the launches traced: 54.7 us -> 47.6 us
  Pallas kernels: 49.2 us -> 43.2 us
  local copies, waits for them, and re-layouts: 4.92 us -> 3.74 us
    pallas_call x1, Pallas kernels: 49.2 us -> 43.2 us  [shards(): pl.pallas_call(functools.partial(kernel, patches, rows * patches), out_sh...]
    unnamed x10 -> x2, local copies, waits for them, and re-layouts: 4.92 us -> 3.74 us
where the time goes in v2:
time: 47.8 us; the launch traced here: 47.6 us
  Pallas kernels  43.2 us (90%)
  local copies, waits for them, and re-layouts  3.74 us (8%)
  between operations  0.64 us (1%)
    pallas_call x1, Pallas kernels, shards(): pl.pallas_call(functools.partial(kernel, patches, rows * patches), out_sh...  43.2 us
    unnamed x2, local copies, waits for them, and re-layouts  3.74 us

profile of v2, /device:TPU:0, one launch (start us, length us, event | category | flops | bytes accessed | tf_op | source)
XLA Modules:
  0.0 47.6 jit_solution(2830084434955615942)
XLA Ops:
  0.6 43.2 %shard_map.68 = (bf16[16,128,128]{2,1,0:T(8,128)(2,1)}, f32[64,2048]{1,0:T(8,128)}) custom-call(bf16[16,128,128]{2,1,0:T(8,128)(2,1)} %bitcast.3, bf16[16,16,128,128]{3,2,1,0:T(8,128)(2,1)} %nf.1, s32[16,16]{1,0:T(8,128)} %ids_in.1, s32[16]{0:T(128)} %counts_in.1, bf16[512,256]{1,0:T(8,128)(2,1)} %psi.1), custom_call_target="tpu_custom_call" | custom-call | tf_op jit(solution)/shard_map/pallas_call | solution.py:344
  43.8 1.9 %copy.9 = bf16[2048,128]{1,0:T(8,128)(2,1)} copy(bf16[2048,128]{1,0:T(8,128)(2,1)} %bitcast.2) | data formatting | bytes 1048576
  45.7 1.9 %copy.10 = f32[64,2048]{1,0:T(8,128)} copy(f32[64,2048]{1,0:T(8,128)} %get-tuple-element.9) | data formatting | bytes 1048576

commit v3 on v2

--- a/solution.py
+++ b/solution.py
@@ -57,8 +57,8 @@
 
 
 def kernel(
-    patches, total_rows, probe, nf, ids_in, counts_in, psi, sample_out, basis_out,
-    win, nfv, ids, counts, idx, psiv, psit, samp, keep, send, crecv, fac, xsend, xrecv, split, gsend, grecv, bas,
+    patches, probe, nf, ids_in, counts_in, psi, sample_out, split_out, packed_out,
+    win, nfv, ids, counts, idx, psiv, psit, samp, keep, send, crecv, fac, xsend, xrecv, split, gsend, grecv,
     hs, hr, ls, nfs, sos, cs, cr, xs, xr, gs, gr, bos,
 ):
     blk_dev, slots, blk, width = nf.shape[0], nf.shape[1], nf.shape[2], probe.shape[2]
@@ -252,6 +252,7 @@
             pass_on(c - 1)
     pass_on(CHUNKS - 1)
 
+    split_copies = []
     gram = jnp.zeros((rank, 2 * rank), F32)
     for c in range(CHUNKS):
         side_copy(c).wait_recv()
@@ -259,6 +260,9 @@
         high = factor.astype(BF16)
         low = (factor - high.astype(F32)).astype(BF16)
         split[c] = jnp.concatenate([high, low, high], 0)
+        copy = pltpu.make_async_copy(split.at[c], split_out.at[c], bos.at[c])
+        copy.start()
+        split_copies.append(copy)
         twice_high = jnp.concatenate([high, high], 0)
         twice_low = jnp.concatenate([low, low], 0)
         both = lax.dot_general(split[c, : 2 * rank], twice_high, NT, preferred_element_type=F32)
@@ -286,9 +290,39 @@
             packed = packed + grecv[slot]
         gram_copies += copies
 
+    packed_out[...] = packed
+
+    near_b.wait_send()
+    near_a.wait_send()
+
+    @pl.when(has_behind)
+    def _():
+        behind_a.wait_send()
+        behind_b.wait_send()
+
+    @pl.when(has_ahead)
+    def _():
+        ahead_a.wait_send()
+        ahead_b.wait_send()
+        relay_a.wait_send()
+        relay_b.wait_send()
+
+    for c in range(CHUNKS):
+        core_copy(c).wait_send()
+        side_copy(c).wait_send()
+        sample_copies[c].wait()
+        split_copies[c].wait()
+    for copy, _ in gram_copies:
+        copy.wait_send()
+
+
+def finish(total_rows, sample, split, packed, sample_out, basis_out, bas, ss, bs):
+    rank, cw = 2 * packed.shape[0], split.shape[2]
+    sample_copy = pltpu.make_async_copy(sample, sample_out, ss.at[0])
+    sample_copy.start()
     lane = lax.broadcasted_iota(jnp.int32, (rank, 2 * rank), 1)
     row = lax.broadcasted_iota(jnp.int32, (rank, 2 * rank), 0)
-    work = jnp.concatenate([pltpu.roll(packed, rank, 1), packed], 0)
+    work = jnp.concatenate([pltpu.roll(packed[...], rank, 1), packed[...]], 0)
     work = jnp.where(lane < rank, jnp.where(lane == row, 1.0, 0.0), work)
     work, pivots = eliminate(work, rank)
     inverse = work[:, :rank] * (lax.rsqrt(pivots) * math.sqrt(total_rows))
@@ -302,32 +336,12 @@
         bas[:, columns] = lax.dot_general(
             inverse, split[c], NN, preferred_element_type=F32
         )
-        copy = pltpu.make_async_copy(bas.at[:, columns], basis_out.at[:, columns], bos.at[c])
+        copy = pltpu.make_async_copy(bas.at[:, columns], basis_out.at[:, columns], bs.at[c])
         copy.start()
         basis_copies.append(copy)
-
-    near_b.wait_send()
-    near_a.wait_send()
-
-    @pl.when(has_behind)
-    def _():
-        behind_a.wait_send()
-        behind_b.wait_send()
-
-    @pl.when(has_ahead)
-    def _():
-        ahead_a.wait_send()
-        ahead_b.wait_send()
-        relay_a.wait_send()
-        relay_b.wait_send()
-
-    for c in range(CHUNKS):
-        core_copy(c).wait_send()
-        side_copy(c).wait_send()
-        sample_copies[c].wait()
-        basis_copies[c].wait()
-    for copy, _ in gram_copies:
-        copy.wait_send()
+    for copy in basis_copies:
+        copy.wait()
+    sample_copy.wait()
 
 
 def shards(probe_columns, near_field, column_ids, block_counts, sketch_matrix):
@@ -341,14 +355,20 @@
     sends = sum(len(stage) for stage in plan)
     anywhere = pl.BlockSpec(memory_space=pltpu.HBM)
     dma = pltpu.SemaphoreType.DMA
-    sample, basis = pl.pallas_call(
-        functools.partial(kernel, patches, rows * patches),
+    operands = (
+        probe_columns.reshape(blk_dev, blk, width), near_field, column_ids, block_counts, sketch_matrix
+    )
+    in_hbm = [pltpu.with_memory_space_constraint(operand, pltpu.HBM) for operand in operands]
+    held = pl.BlockSpec(memory_space=pltpu.VMEM)
+    sample, split, packed = pl.pallas_call(
+        functools.partial(kernel, patches),
         out_shape=[
             jax.ShapeDtypeStruct((blk_dev, blk, width), BF16),
-            jax.ShapeDtypeStruct((rank, rows), F32),
+            jax.ShapeDtypeStruct((CHUNKS, 3 * rank, cw), BF16),
+            jax.ShapeDtypeStruct((rank // 2, 2 * rank), F32),
         ],
         in_specs=[anywhere] * 5,
-        out_specs=[anywhere, anywhere],
+        out_specs=[anywhere, anywhere, held],
         scratch_shapes=[
             pltpu.VMEM(((2 * REACH + 1) * blk_dev + 1, blk, width), BF16),
             pltpu.VMEM(near_field.shape, BF16),
@@ -367,18 +387,25 @@
             pltpu.VMEM((CHUNKS, 3 * rank, cw), BF16),
             pltpu.VMEM((len(plan), rank // 2, 2 * rank), F32),
             pltpu.VMEM((sends, rank // 2, 2 * rank), F32),
-            pltpu.VMEM((rank, rows), F32),
             dma((8,)), dma((8,)), dma((4,)), dma((CHUNKS,)), dma((CHUNKS,)),
             dma((CHUNKS,)), dma((CHUNKS,)), dma((CHUNKS,)), dma((CHUNKS,)),
             dma((sends,)), dma((sends,)), dma((CHUNKS,)),
         ],
         compiler_params=pltpu.CompilerParams(
-            collective_id=0, has_side_effects=True, vmem_limit_bytes=64 * 2**20
+            collective_id=0, has_side_effects=True, vmem_limit_bytes=48 * 2**20
         ),
-    )(
-        probe_columns.reshape(blk_dev, blk, width), near_field, column_ids, block_counts,
-        sketch_matrix,
-    )
+    )(*in_hbm)
+    sample, basis = pl.pallas_call(
+        functools.partial(finish, rows * patches),
+        out_shape=[
+            jax.ShapeDtypeStruct((blk_dev, blk, width), BF16),
+            jax.ShapeDtypeStruct((rank, rows), F32),
+        ],
+        in_specs=[anywhere, held, held],
+        out_specs=[anywhere, anywhere],
+        scratch_shapes=[pltpu.VMEM((rank, rows), F32), dma((1,)), dma((CHUNKS,))],
+        compiler_params=pltpu.CompilerParams(vmem_limit_bytes=16 * 2**20),
+    )(sample, split, packed)
     return (sample.reshape(rows, width), basis)
 
 

time: 47.8 us -> 45.4 us (0.950)
  local copies, waits for them, and re-layouts: 3.74 us -> 0 us
  Pallas kernels: 43.2 us -> 44.6 us
    unnamed x2 -> x0, local copies, waits for them, and re-layouts: 3.74 us -> none
    pallas_call x1 -> x2, Pallas kernels: 43.2 us -> 44.6 us  [the longest x1 41.7 us: shards(): pl.pallas_call(functools.partial(kernel, patches), out_shape=[jax.ShapeDt...]
where the time goes in v3:
time: 45.4 us; the launch traced here: 45.2 us
  Pallas kernels  44.6 us (98%)
  between operations  0.64 us (1%)
    pallas_call x1, Pallas kernels, shards(): pl.pallas_call(functools.partial(kernel, patches), out_shape=[jax.ShapeDt...  41.7 us
    pallas_call x1, Pallas kernels, shards(): pl.pallas_call(functools.partial(finish, rows * patches), out_shape=[jax....  2.91 us

profile of v3, /device:TPU:0, one launch (start us, length us, event | category | flops | bytes accessed | tf_op | source)
XLA Modules:
  0.0 45.2 jit_solution(13233699483012609639)
XLA Ops:
  0.6 41.7 %shard_map.68 = (bf16[16,128,128]{2,1,0:T(8,128)(2,1)S(1)}, bf16[4,192,512]{2,1,0:T(8,128)(2,1)S(1)}, f32[32,128]{1,0:T(8,128)S(1)}) custom-call(bf16[16,128,128]{2,1,0:T(8,128)(2,1)} %bitcast.2, bf16[16,16,128,128]{3,2,1,0:T(8,128)(2,1)} %nf.1, s32[16,16]{1,0:T(8,128)} %ids_in.1, s32[16]{0:T(128)} %counts_in.1, bf16[512,256]{1,0:T(8,128)(2,1)} %psi.1), custom_call_target="tpu_custom_call" | custom-call | tf_op jit(solution)/shard_map/pallas_call | solution.py:363
  42.3 2.9 %shard_map.69 = (bf16[16,128,128]{2,1,0:T(8,128)(2,1)}, f32[64,2048]{1,0:T(8,128)}) custom-call(bf16[16,128,128]{2,1,0:T(8,128)(2,1)S(1)} %get-tuple-element.7.sample, bf16[4,192,512]{2,1,0:T(8,128)(2,1)S(1)} %get-tuple-element.8.split, f32[32,128]{1,0:T(8,128)S(1)} %get-tuple-element.9.packed), custom_call_target="tpu_custom_call" | custom-call | tf_op jit(solution)/shard_map/pallas_call | solution.py:398
